TPU v7x, 1024 devices: a whole 4x4x32 slice. The times are simulated.
1024 devices in a mesh: gx: 32 (over z), gy: 8 (over y, x_lo), gz: 4 (over x_hi, core).
Axes of the slice: x: 4 (x_hi: 2, x_lo: 2; x = x_hi * 2 + x_lo), y: 4, z: 32, core: 2. Of those that a mesh axis runs over, the one named last changes fastest.
Arguments:
- load_parts: float32 [32, 8, 4, 602, 128], P('gx', 'gy', 'gz'), may hold values from -6 to 6
- schur_blocks: bfloat16 [32, 8, 4, 602, 602], P('gx', 'gy', 'gz'), may hold values from -0.13 to 3, as said below
- dirichlet_blocks: bfloat16 [32, 8, 4, 602, 602], P('gx', 'gy', 'gz'), may hold values from -0.06 to 1, as said below
- node_order: int32 [32, 8, 4, 602], P('gx', 'gy', 'gz'), may hold values from 0 to 1330, as said below
Outputs:
- solution: float32 [32, 8, 4, 602, 128], P('gx', 'gy', 'gz')
- residual: float32 [32, 8, 4, 602, 128], P('gx', 'gy', 'gz')
Inputs may be any that keep to these rules, and one draw needn't show every extreme that they name: `node_order`: each subdomain's row lists every surface position of its 11 x 11 x 11 block exactly once, in an order of its own. `schur_blocks`: each subdomain's block is symmetric. `dirichlet_blocks`: each subdomain's block is symmetric.
All inputs are finite; a program needn't handle non-finite values.
Results may differ from a plain program's by a relative error of at most 0.007.
Values sent between devices are 32-bit elements; how exact they have to be, the bound alone decides.
A program may use at most 32 MiB of HBM per device.

v0:
```python
import jax
import jax.numpy as jnp
from jax import lax
from jax.sharding import PartitionSpec as P

NODES = 11
ITERS = 2


spectrum_low = 0.3
spectrum_high = 5.0


def with_halo(value, sides, width):
    for axis, dim in sides:
        peers, length = (lax.axis_size(axis), value.shape[dim])
        up = [(i, (i + 1) % peers) for i in range(peers - 1)]
        down = [(j, i) for i, j in up]
        last = lax.slice_in_dim(value, length - width, length, axis=dim)
        leading = lax.slice_in_dim(value, 0, width, axis=dim)
        before = lax.ppermute(last, axis, up)
        after = lax.ppermute(leading, axis, down)
        value = jnp.concatenate([before, value, after], axis=dim)
    return value


def node_counts(axis_name_count, axis_place):
    places = jnp.arange(NODES)
    lower = ((places == 0) & (axis_place > 0)).astype(jnp.float32)
    upper = ((places == NODES - 1) & (axis_place < axis_name_count - 1)).astype(jnp.float32)
    return 1.0 + lower + upper


def fold_dim(padded, dim):
    length = padded.shape[dim] - 2
    low_face = lax.slice_in_dim(padded, 0, 1, axis=dim) + lax.slice_in_dim(padded, 1, 2, axis=dim)
    middle = lax.slice_in_dim(padded, 2, length, axis=dim)
    high_face = lax.slice_in_dim(padded, length, length + 1, axis=dim) + lax.slice_in_dim(
        padded, length + 1, length + 2, axis=dim
    )
    return jnp.concatenate([low_face, middle, high_face], axis=dim)


def link_cube(cube_field):
    padded = with_halo(cube_field, (("gx", 0), ("gy", 1), ("gz", 2)), 1)
    joined = fold_dim(padded, 0)
    joined = fold_dim(joined, 1)
    return fold_dim(joined, 2)


def on_device(load_parts, schur_blocks, dirichlet_blocks, node_order):
    numbering = node_order.reshape(-1)
    iface_count = numbering.shape[0]
    columns = load_parts.shape[-1]
    schur_local = schur_blocks.reshape(iface_count, iface_count)
    dirichlet_local = dirichlet_blocks.reshape(iface_count, iface_count)
    loads = load_parts.reshape(iface_count, columns)
    count_x = node_counts(lax.axis_size("gx"), lax.axis_index("gx"))
    count_y = node_counts(lax.axis_size("gy"), lax.axis_index("gy"))
    count_z = node_counts(lax.axis_size("gz"), lax.axis_index("gz"))
    mult = (count_x[:, None, None] * count_y[None, :, None] * count_z[None, None, :]).reshape(
        NODES**3
    )
    weight = (1.0 / mult[numbering])[:, None]

    def assemble(vectors):
        cube_field = (
            jnp.zeros((NODES**3, columns), jnp.float32)
            .at[numbering]
            .set(vectors, unique_indices=True)
        )
        cube_field = cube_field.reshape(NODES, NODES, NODES, columns)
        joined = link_cube(cube_field)
        return joined.reshape(NODES**3, columns)[numbering]

    def precondition(vectors):
        product = jnp.dot(
            dirichlet_local,
            (weight * vectors).astype(jnp.bfloat16),
            preferred_element_type=jnp.float32,
        )
        return weight * assemble(product)

    theta = (spectrum_high + spectrum_low) / 2.0
    delta = (spectrum_high - spectrum_low) / 2.0
    sigma = theta / delta
    solution = jnp.zeros_like(loads)
    residual = assemble(loads)
    rho_now = 1.0 / sigma
    direction = precondition(residual) / theta
    for index in range(ITERS):
        product = jnp.dot(
            schur_local, direction.astype(jnp.bfloat16), preferred_element_type=jnp.float32
        )
        image = assemble(product)
        solution = solution + direction
        residual = residual - image
        if index + 1 < ITERS:
            rho_next = 1.0 / (2.0 * sigma - rho_now)
            direction = rho_next * rho_now * direction + 2.0 * rho_next / delta * precondition(
                residual
            )
            rho_now = rho_next
    out_shape = load_parts.shape
    return (solution.reshape(out_shape), residual.reshape(out_shape))


def solution(mesh):
    in_specs = (
        P("gx", "gy", "gz", None, None),
        P("gx", "gy", "gz", None, None),
        P("gx", "gy", "gz", None, None),
        P("gx", "gy", "gz", None),
    )
    out_specs = (P("gx", "gy", "gz", None, None), P("gx", "gy", "gz", None, None))
    return jax.shard_map(
        on_device, mesh=mesh, in_specs=in_specs, out_specs=out_specs, check_vma=False
    )
```

profile of v0, /device:TPU:161, one launch (start us, length us, event | category | flops | bytes accessed | tf_op | source)
XLA Modules:
  0.0 206.3 jit_solution(4247461067830402968)
XLA Ops:
  1.4 4.9 %scatter_custom_fusion = f32[1331,128]{1,0:T(8,128)S(1)} fusion(s32[602]{0:T(1024)S(1)} %fusion.26, f32[]{:T(128)} %constant.37.clone.1, f32[1,1,1,602,128]{4,2,3,1,0:T(1,128)} %param.4), kind=kCustom, calls=%fused_computation.47 | custom fusion | bytes 989700 | tf_op jit(solution)/shard_map/scatter | solution.py:70
  19.8 3.9 %gather_fusion = f32[602]{0:T(1024)S(1)} fusion(f32[1331]{0:T(1024)S(1)} %mul.121, s32[1024]{0:T(1024)S(1)} %pad_clamp_fusion), kind=kCustom, calls=%fused_computation | custom fusion | bytes 7224 | tf_op jit(solution)/shard_map/gather | solution.py:64
  25.0 6.7 %collective-permute-start.4 = (f32[13,13,1,128]{3,2,1,0:T(1,128)S(1)}, f32[13,13,1,128]{3,2,1,0:T(1,128)S(1)}, u32[]{:S(2)}, u32[]{:S(2)}) collective-permute-start(f32[13,13,1,128]{3,2,1,0:T(1,128)S(1)} %get-tuple-element.14), channel_id=1, source_target_pairs={{0,1},{1,2},{2,3},{4,5},{5,6},{6,7},{8,9},{9,10},{10,11},{12,13},{... | collective-permute-start | bytes 259592 | tf_op jit(solution)/shard_map/ppermute | solution.py:21
  33.7 5.4 %collective-permute-done.5 = f32[13,13,1,128]{3,2,1,0:T(1,128)S(1)} collective-permute-done((f32[13,13,1,128]{3,2,1,0:T(1,128)S(1)}, f32[13,13,1,128]{3,2,1,0:T(1,128)S(1)}, u32[]{:S(2)}, u32[]{:S(2)}) %collective-permute-start.5) | collective-permute-done | bytes 86560 | tf_op jit(solution)/shard_map/ppermute | solution.py:22
  43.2 4.3 %scatter_custom_fusion.1 = f32[1331,128]{1,0:T(8,128)S(1)} fusion(s32[602]{0:T(1024)S(1)} %fusion.26, f32[602,128]{1,0:T(8,128)S(1)} %convolution_bitcast_fusion.3, f32[]{:T(128)} %constant.37.clone.1), kind=kCustom, calls=%fused_computation.45 | custom fusion | bytes 681476 | tf_op jit(solution)/shard_map/scatter | solution.py:70
  47.6 4.7 %collective-permute-start.6 = (f32[1,11,11,128]{3,2,1,0:T(8,128)S(1)}, f32[1,11,11,128]{3,2,1,0:T(8,128)S(1)}, u32[]{:S(2)}, u32[]{:S(2)}) collective-permute-start(f32[1,11,11,128]{3,2,1,0:T(8,128)S(1)} %slice.369), channel_id=1, source_target_pairs={{0,32},{32,64},{64,96},{96,128},{128,160},{160,192},{192,224},{224... | collective-permute-start | bytes 185864 | tf_op jit(solution)/shard_map/ppermute | solution.py:21
  54.4 4.7 %collective-permute-done.7 = f32[1,11,11,128]{3,2,1,0:T(8,128)S(1)} collective-permute-done((f32[1,11,11,128]{3,2,1,0:T(8,128)S(1)}, f32[1,11,11,128]{3,2,1,0:T(8,128)S(1)}, u32[]{:S(2)}, u32[]{:S(2)}) %collective-permute-start.7) | collective-permute-done | bytes 61984 | tf_op jit(solution)/shard_map/ppermute | solution.py:22
  59.1 3.8 %collective-permute-start.8 = (f32[13,1,11,128]{3,2,1,0:T(8,128)S(1)}, f32[13,1,11,128]{3,2,1,0:T(8,128)S(1)}, u32[]{:S(2)}, u32[]{:S(2)}) collective-permute-start(f32[13,1,11,128]{3,2,1,0:T(8,128)S(1)} %get-tuple-element.30), channel_id=1, source_target_pairs={{0,4},{4,8},{8,12},{12,16},{16,20},{20,24},{24,28},{1,5},{5,9},{9,... | collective-permute-start | bytes 219656 | tf_op jit(solution)/shard_map/ppermute | solution.py:21
  64.6 3.9 %collective-permute-done.9 = f32[13,1,11,128]{3,2,1,0:T(8,128)S(1)} collective-permute-done((f32[13,1,11,128]{3,2,1,0:T(8,128)S(1)}, f32[13,1,11,128]{3,2,1,0:T(8,128)S(1)}, u32[]{:S(2)}, u32[]{:S(2)}) %collective-permute-start.9) | collective-permute-done | bytes 73248 | tf_op jit(solution)/shard_map/ppermute | solution.py:22
  68.6 4.9 %collective-permute-start.10 = (f32[13,13,1,128]{3,2,1,0:T(1,128)S(1)}, f32[13,13,1,128]{3,2,1,0:T(1,128)S(1)}, u32[]{:S(2)}, u32[]{:S(2)}) collective-permute-start(f32[13,13,1,128]{3,2,1,0:T(1,128)S(1)} %get-tuple-element.12), channel_id=1, source_target_pairs={{0,1},{1,2},{2,3},{4,5},{5,6},{6,7},{8,9},{9,10},{10,11},{12,13},{... | collective-permute-start | bytes 259592 | tf_op jit(solution)/shard_map/ppermute | solution.py:21
  75.6 5.2 %collective-permute-done.11 = f32[13,13,1,128]{3,2,1,0:T(1,128)S(1)} collective-permute-done((f32[13,13,1,128]{3,2,1,0:T(1,128)S(1)}, f32[13,13,1,128]{3,2,1,0:T(1,128)S(1)}, u32[]{:S(2)}, u32[]{:S(2)}) %collective-permute-start.11) | collective-permute-done | bytes 86560 | tf_op jit(solution)/shard_map/ppermute | solution.py:22
  84.3 4.3 %scatter_custom_fusion.2 = f32[1331,128]{1,0:T(8,128)S(1)} fusion(s32[602]{0:T(1024)S(1)} %fusion.26, f32[602,128]{1,0:T(8,128)S(1)} %convolution_bitcast_fusion.2, f32[]{:T(128)} %constant.37.clone.1), kind=kCustom, calls=%fused_computation.43 | custom fusion | bytes 681476 | tf_op jit(solution)/shard_map/scatter | solution.py:70
  104.8 3.9 %collective-permute-done.15 = f32[13,1,11,128]{3,2,1,0:T(8,128)S(1)} collective-permute-done((f32[13,1,11,128]{3,2,1,0:T(8,128)S(1)}, f32[13,1,11,128]{3,2,1,0:T(8,128)S(1)}, u32[]{:S(2)}, u32[]{:S(2)}) %collective-permute-start.15) | collective-permute-done | bytes 73248 | tf_op jit(solution)/shard_map/ppermute | solution.py:22
  108.8 5.0 %collective-permute-start.16 = (f32[13,13,1,128]{3,2,1,0:T(1,128)S(1)}, f32[13,13,1,128]{3,2,1,0:T(1,128)S(1)}, u32[]{:S(2)}, u32[]{:S(2)}) collective-permute-start(f32[13,13,1,128]{3,2,1,0:T(1,128)S(1)} %get-tuple-element.10), channel_id=1, source_target_pairs={{0,1},{1,2},{2,3},{4,5},{5,6},{6,7},{8,9},{9,10},{10,11},{12,13},{... | collective-permute-start | bytes 259592 | tf_op jit(solution)/shard_map/ppermute | solution.py:21
  115.8 5.4 %collective-permute-done.17 = f32[13,13,1,128]{3,2,1,0:T(1,128)S(1)} collective-permute-done((f32[13,13,1,128]{3,2,1,0:T(1,128)S(1)}, f32[13,13,1,128]{3,2,1,0:T(1,128)S(1)}, u32[]{:S(2)}, u32[]{:S(2)}) %collective-permute-start.17) | collective-permute-done | bytes 86560 | tf_op jit(solution)/shard_map/ppermute | solution.py:22
  125.4 4.3 %scatter_custom_fusion.3 = f32[1331,128]{1,0:T(8,128)S(1)} fusion(s32[602]{0:T(1024)S(1)} %fusion.26, f32[602,128]{1,0:T(8,128)S(1)} %convolution_bitcast_fusion.1, f32[]{:T(128)} %constant.37.clone.1), kind=kCustom, calls=%fused_computation.41 | custom fusion | bytes 681476 | tf_op jit(solution)/shard_map/scatter | solution.py:70
  146.5 3.9 %collective-permute-done.21 = f32[13,1,11,128]{3,2,1,0:T(8,128)S(1)} collective-permute-done((f32[13,1,11,128]{3,2,1,0:T(8,128)S(1)}, f32[13,1,11,128]{3,2,1,0:T(8,128)S(1)}, u32[]{:S(2)}, u32[]{:S(2)}) %collective-permute-start.21) | collective-permute-done | bytes 73248 | tf_op jit(solution)/shard_map/ppermute | solution.py:22
  150.5 4.9 %collective-permute-start.22 = (f32[13,13,1,128]{3,2,1,0:T(1,128)S(1)}, f32[13,13,1,128]{3,2,1,0:T(1,128)S(1)}, u32[]{:S(2)}, u32[]{:S(2)}) collective-permute-start(f32[13,13,1,128]{3,2,1,0:T(1,128)S(1)} %get-tuple-element.8), channel_id=1, source_target_pairs={{0,1},{1,2},{2,3},{4,5},{5,6},{6,7},{8,9},{9,10},{10,11},{12,13},{... | collective-permute-start | bytes 259592 | tf_op jit(solution)/shard_map/ppermute | solution.py:21
  157.6 5.2 %collective-permute-done.23 = f32[13,13,1,128]{3,2,1,0:T(1,128)S(1)} collective-permute-done((f32[13,13,1,128]{3,2,1,0:T(1,128)S(1)}, f32[13,13,1,128]{3,2,1,0:T(1,128)S(1)}, u32[]{:S(2)}, u32[]{:S(2)}) %collective-permute-start.23) | collective-permute-done | bytes 86560 | tf_op jit(solution)/shard_map/ppermute | solution.py:22
  166.2 4.3 %scatter_custom_fusion.4 = f32[1331,128]{1,0:T(8,128)S(1)} fusion(s32[602]{0:T(1024)S(1)} %fusion.26, f32[602,128]{1,0:T(8,128)S(1)} %convolution_bitcast_fusion, f32[]{:T(128)} %constant.37.clone.1), kind=kCustom, calls=%fused_computation.39 | custom fusion | bytes 681476 | tf_op jit(solution)/shard_map/scatter | solution.py:70
  176.4 4.7 %collective-permute-done.25 = f32[1,11,11,128]{3,2,1,0:T(8,128)S(1)} collective-permute-done((f32[1,11,11,128]{3,2,1,0:T(8,128)S(1)}, f32[1,11,11,128]{3,2,1,0:T(8,128)S(1)}, u32[]{:S(2)}, u32[]{:S(2)}) %collective-permute-start.25) | collective-permute-done | bytes 61984 | tf_op jit(solution)/shard_map/ppermute | solution.py:22
  186.0 3.8 %collective-permute-done.27 = f32[13,1,11,128]{3,2,1,0:T(8,128)S(1)} collective-permute-done((f32[13,1,11,128]{3,2,1,0:T(8,128)S(1)}, f32[13,1,11,128]{3,2,1,0:T(8,128)S(1)}, u32[]{:S(2)}, u32[]{:S(2)}) %collective-permute-start.27) | collective-permute-done | bytes 73248 | tf_op jit(solution)/shard_map/ppermute | solution.py:22
  189.9 5.0 %collective-permute-start.28 = (f32[13,13,1,128]{3,2,1,0:T(1,128)S(1)}, f32[13,13,1,128]{3,2,1,0:T(1,128)S(1)}, u32[]{:S(2)}, u32[]{:S(2)}) collective-permute-start(f32[13,13,1,128]{3,2,1,0:T(1,128)S(1)} %get-tuple-element.6), channel_id=1, source_target_pairs={{0,1},{1,2},{2,3},{4,5},{5,6},{6,7},{8,9},{9,10},{10,11},{12,13},{... | collective-permute-start | bytes 259592 | tf_op jit(solution)/shard_map/ppermute | solution.py:21
  198.1 4.2 %collective-permute-done.29 = f32[13,13,1,128]{3,2,1,0:T(1,128)S(1)} collective-permute-done((f32[13,13,1,128]{3,2,1,0:T(1,128)S(1)}, f32[13,13,1,128]{3,2,1,0:T(1,128)S(1)}, u32[]{:S(2)}, u32[]{:S(2)}) %collective-permute-start.29) | collective-permute-done | bytes 86560 | tf_op jit(solution)/shard_map/ppermute | solution.py:22
  (185 shorter events, 93.3 us)
Async XLA Ops:
  6.3 6.0 %collective-permute-start = (f32[1,11,11,128]{3,2,1,0:T(8,128)S(1)}, f32[1,11,11,128]{3,2,1,0:T(8,128)S(1)}, u32[]{:S(2)}, u32[]{:S(2)}) collective-permute-start(f32[1,11,11,128]{3,2,1,0:T(8,128)S(1)} %slice.346), channel_id=1, source_target_pairs={{0,32},{32,64},{64,96},{96,128},{128,160},{160,192},{192,224},{224... | collective-permute-start | bytes 185864 | tf_op jit(solution)/shard_map/ppermute | solution.py:21
  15.4 8.3 %collective-permute-start.2 = (f32[13,1,11,128]{3,2,1,0:T(8,128)S(1)}, f32[13,1,11,128]{3,2,1,0:T(8,128)S(1)}, u32[]{:S(2)}, u32[]{:S(2)}) collective-permute-start(f32[13,1,11,128]{3,2,1,0:T(8,128)S(1)} %get-tuple-element.34), channel_id=1, source_target_pairs={{0,4},{4,8},{8,12},{12,16},{16,20},{20,24},{24,28},{1,5},{5,9},{9,... | collective-permute-start | bytes 219656 | tf_op jit(solution)/shard_map/ppermute | solution.py:21
  18.5 6.3 %collective-permute-start.3 = (f32[13,1,11,128]{3,2,1,0:T(8,128)S(1)}, f32[13,1,11,128]{3,2,1,0:T(8,128)S(1)}, u32[]{:S(2)}, u32[]{:S(2)}) collective-permute-start(f32[13,1,11,128]{3,2,1,0:T(8,128)S(1)} %get-tuple-element.35), channel_id=1, source_target_pairs={{4,0},{8,4},{12,8},{16,12},{20,16},{24,20},{28,24},{5,1},{9,5},{13... | collective-permute-start | bytes 219656 | tf_op jit(solution)/shard_map/ppermute | solution.py:22
  25.0 8.7 %collective-permute-start.4 = (f32[13,13,1,128]{3,2,1,0:T(1,128)S(1)}, f32[13,13,1,128]{3,2,1,0:T(1,128)S(1)}, u32[]{:S(2)}, u32[]{:S(2)}) collective-permute-start(f32[13,13,1,128]{3,2,1,0:T(1,128)S(1)} %get-tuple-element.14), channel_id=1, source_target_pairs={{0,1},{1,2},{2,3},{4,5},{5,6},{6,7},{8,9},{9,10},{10,11},{12,13},{... | collective-permute-start | bytes 259592 | tf_op jit(solution)/shard_map/ppermute | solution.py:21
  31.7 7.3 %collective-permute-start.5 = (f32[13,13,1,128]{3,2,1,0:T(1,128)S(1)}, f32[13,13,1,128]{3,2,1,0:T(1,128)S(1)}, u32[]{:S(2)}, u32[]{:S(2)}) collective-permute-start(f32[13,13,1,128]{3,2,1,0:T(1,128)S(1)} %get-tuple-element.15), channel_id=1, source_target_pairs={{1,0},{2,1},{3,2},{5,4},{6,5},{7,6},{9,8},{10,9},{11,10},{13,12},{... | collective-permute-start | bytes 259592 | tf_op jit(solution)/shard_map/ppermute | solution.py:22
  47.6 6.7 %collective-permute-start.6 = (f32[1,11,11,128]{3,2,1,0:T(8,128)S(1)}, f32[1,11,11,128]{3,2,1,0:T(8,128)S(1)}, u32[]{:S(2)}, u32[]{:S(2)}) collective-permute-start(f32[1,11,11,128]{3,2,1,0:T(8,128)S(1)} %slice.369), channel_id=1, source_target_pairs={{0,32},{32,64},{64,96},{96,128},{128,160},{160,192},{192,224},{224... | collective-permute-start | bytes 185864 | tf_op jit(solution)/shard_map/ppermute | solution.py:21
  52.3 6.8 %collective-permute-start.7 = (f32[1,11,11,128]{3,2,1,0:T(8,128)S(1)}, f32[1,11,11,128]{3,2,1,0:T(8,128)S(1)}, u32[]{:S(2)}, u32[]{:S(2)}) collective-permute-start(f32[1,11,11,128]{3,2,1,0:T(8,128)S(1)} %slice.371), channel_id=1, source_target_pairs={{32,0},{64,32},{96,64},{128,96},{160,128},{192,160},{224,192},{256... | collective-permute-start | bytes 185864 | tf_op jit(solution)/shard_map/ppermute | solution.py:22
  59.1 5.5 %collective-permute-start.8 = (f32[13,1,11,128]{3,2,1,0:T(8,128)S(1)}, f32[13,1,11,128]{3,2,1,0:T(8,128)S(1)}, u32[]{:S(2)}, u32[]{:S(2)}) collective-permute-start(f32[13,1,11,128]{3,2,1,0:T(8,128)S(1)} %get-tuple-element.30), channel_id=1, source_target_pairs={{0,4},{4,8},{8,12},{12,16},{16,20},{20,24},{24,28},{1,5},{5,9},{9,... | collective-permute-start | bytes 219656 | tf_op jit(solution)/shard_map/ppermute | solution.py:21
  62.9 5.6 %collective-permute-start.9 = (f32[13,1,11,128]{3,2,1,0:T(8,128)S(1)}, f32[13,1,11,128]{3,2,1,0:T(8,128)S(1)}, u32[]{:S(2)}, u32[]{:S(2)}) collective-permute-start(f32[13,1,11,128]{3,2,1,0:T(8,128)S(1)} %get-tuple-element.31), channel_id=1, source_target_pairs={{4,0},{8,4},{12,8},{16,12},{20,16},{24,20},{28,24},{5,1},{9,5},{13... | collective-permute-start | bytes 219656 | tf_op jit(solution)/shard_map/ppermute | solution.py:22
  68.6 7.0 %collective-permute-start.10 = (f32[13,13,1,128]{3,2,1,0:T(1,128)S(1)}, f32[13,13,1,128]{3,2,1,0:T(1,128)S(1)}, u32[]{:S(2)}, u32[]{:S(2)}) collective-permute-start(f32[13,13,1,128]{3,2,1,0:T(1,128)S(1)} %get-tuple-element.12), channel_id=1, source_target_pairs={{0,1},{1,2},{2,3},{4,5},{5,6},{6,7},{8,9},{9,10},{10,11},{12,13},{... | collective-permute-start | bytes 259592 | tf_op jit(solution)/shard_map/ppermute | solution.py:21
  73.5 7.3 %collective-permute-start.11 = (f32[13,13,1,128]{3,2,1,0:T(1,128)S(1)}, f32[13,13,1,128]{3,2,1,0:T(1,128)S(1)}, u32[]{:S(2)}, u32[]{:S(2)}) collective-permute-start(f32[13,13,1,128]{3,2,1,0:T(1,128)S(1)} %get-tuple-element.13), channel_id=1, source_target_pairs={{1,0},{2,1},{3,2},{5,4},{6,5},{7,6},{9,8},{10,9},{11,10},{13,12},{... | collective-permute-start | bytes 259592 | tf_op jit(solution)/shard_map/ppermute | solution.py:22
  89.9 6.5 %collective-permute-start.12 = (f32[1,11,11,128]{3,2,1,0:T(8,128)}, f32[1,11,11,128]{3,2,1,0:T(8,128)}, u32[]{:S(2)}, u32[]{:S(2)}) collective-permute-start(f32[1,11,11,128]{3,2,1,0:T(8,128)} %slice.392), channel_id=1, source_target_pairs={{0,32},{32,64},{64,96},{96,128},{128,160},{160,192},{192,224},{224... | collective-permute-start | bytes 185864 | tf_op jit(solution)/shard_map/ppermute | solution.py:21
  103.1 5.6 %collective-permute-start.15 = (f32[13,1,11,128]{3,2,1,0:T(8,128)S(1)}, f32[13,1,11,128]{3,2,1,0:T(8,128)S(1)}, u32[]{:S(2)}, u32[]{:S(2)}) collective-permute-start(f32[13,1,11,128]{3,2,1,0:T(8,128)S(1)} %get-tuple-element.27), channel_id=1, source_target_pairs={{4,0},{8,4},{12,8},{16,12},{20,16},{24,20},{28,24},{5,1},{9,5},{13... | collective-permute-start | bytes 219656 | tf_op jit(solution)/shard_map/ppermute | solution.py:22
  108.8 6.9 %collective-permute-start.16 = (f32[13,13,1,128]{3,2,1,0:T(1,128)S(1)}, f32[13,13,1,128]{3,2,1,0:T(1,128)S(1)}, u32[]{:S(2)}, u32[]{:S(2)}) collective-permute-start(f32[13,13,1,128]{3,2,1,0:T(1,128)S(1)} %get-tuple-element.10), channel_id=1, source_target_pairs={{0,1},{1,2},{2,3},{4,5},{5,6},{6,7},{8,9},{9,10},{10,11},{12,13},{... | collective-permute-start | bytes 259592 | tf_op jit(solution)/shard_map/ppermute | solution.py:21
  113.9 7.3 %collective-permute-start.17 = (f32[13,13,1,128]{3,2,1,0:T(1,128)S(1)}, f32[13,13,1,128]{3,2,1,0:T(1,128)S(1)}, u32[]{:S(2)}, u32[]{:S(2)}) collective-permute-start(f32[13,13,1,128]{3,2,1,0:T(1,128)S(1)} %get-tuple-element.11), channel_id=1, source_target_pairs={{1,0},{2,1},{3,2},{5,4},{6,5},{7,6},{9,8},{10,9},{11,10},{13,12},{... | collective-permute-start | bytes 259592 | tf_op jit(solution)/shard_map/ppermute | solution.py:22
  131.0 6.4 %collective-permute-start.18 = (f32[1,11,11,128]{3,2,1,0:T(8,128)}, f32[1,11,11,128]{3,2,1,0:T(8,128)}, u32[]{:S(2)}, u32[]{:S(2)}) collective-permute-start(f32[1,11,11,128]{3,2,1,0:T(8,128)} %slice.415), channel_id=1, source_target_pairs={{0,32},{32,64},{64,96},{96,128},{128,160},{160,192},{192,224},{224... | collective-permute-start | bytes 185864 | tf_op jit(solution)/shard_map/ppermute | solution.py:21
  135.5 6.5 %collective-permute-start.19 = (f32[1,11,11,128]{3,2,1,0:T(8,128)S(1)}, f32[1,11,11,128]{3,2,1,0:T(8,128)S(1)}, u32[]{:S(2)}, u32[]{:S(2)}) collective-permute-start(f32[1,11,11,128]{3,2,1,0:T(8,128)S(1)} %slice.417), channel_id=1, source_target_pairs={{32,0},{64,32},{96,64},{128,96},{160,128},{192,160},{224,192},{256... | collective-permute-start | bytes 185864 | tf_op jit(solution)/shard_map/ppermute | solution.py:22
  144.8 5.6 %collective-permute-start.21 = (f32[13,1,11,128]{3,2,1,0:T(8,128)S(1)}, f32[13,1,11,128]{3,2,1,0:T(8,128)S(1)}, u32[]{:S(2)}, u32[]{:S(2)}) collective-permute-start(f32[13,1,11,128]{3,2,1,0:T(8,128)S(1)} %get-tuple-element.23), channel_id=1, source_target_pairs={{4,0},{8,4},{12,8},{16,12},{20,16},{24,20},{28,24},{5,1},{9,5},{13... | collective-permute-start | bytes 219656 | tf_op jit(solution)/shard_map/ppermute | solution.py:22
  150.5 7.1 %collective-permute-start.22 = (f32[13,13,1,128]{3,2,1,0:T(1,128)S(1)}, f32[13,13,1,128]{3,2,1,0:T(1,128)S(1)}, u32[]{:S(2)}, u32[]{:S(2)}) collective-permute-start(f32[13,13,1,128]{3,2,1,0:T(1,128)S(1)} %get-tuple-element.8), channel_id=1, source_target_pairs={{0,1},{1,2},{2,3},{4,5},{5,6},{6,7},{8,9},{9,10},{10,11},{12,13},{... | collective-permute-start | bytes 259592 | tf_op jit(solution)/shard_map/ppermute | solution.py:21
  155.4 7.3 %collective-permute-start.23 = (f32[13,13,1,128]{3,2,1,0:T(1,128)S(1)}, f32[13,13,1,128]{3,2,1,0:T(1,128)S(1)}, u32[]{:S(2)}, u32[]{:S(2)}) collective-permute-start(f32[13,13,1,128]{3,2,1,0:T(1,128)S(1)} %get-tuple-element.9), channel_id=1, source_target_pairs={{1,0},{2,1},{3,2},{5,4},{6,5},{7,6},{9,8},{10,9},{11,10},{13,12},{... | collective-permute-start | bytes 259592 | tf_op jit(solution)/shard_map/ppermute | solution.py:22
  170.6 5.7 %collective-permute-start.24 = (f32[1,11,11,128]{3,2,1,0:T(8,128)S(1)}, f32[1,11,11,128]{3,2,1,0:T(8,128)S(1)}, u32[]{:S(2)}, u32[]{:S(2)}) collective-permute-start(f32[1,11,11,128]{3,2,1,0:T(8,128)S(1)} %slice.438), channel_id=1, source_target_pairs={{0,32},{32,64},{64,96},{96,128},{128,160},{160,192},{192,224},{224... | collective-permute-start | bytes 185864 | tf_op jit(solution)/shard_map/ppermute | solution.py:21
  174.3 6.8 %collective-permute-start.25 = (f32[1,11,11,128]{3,2,1,0:T(8,128)S(1)}, f32[1,11,11,128]{3,2,1,0:T(8,128)S(1)}, u32[]{:S(2)}, u32[]{:S(2)}) collective-permute-start(f32[1,11,11,128]{3,2,1,0:T(8,128)S(1)} %slice.440), channel_id=1, source_target_pairs={{32,0},{64,32},{96,64},{128,96},{160,128},{192,160},{224,192},{256... | collective-permute-start | bytes 185864 | tf_op jit(solution)/shard_map/ppermute | solution.py:22
  189.9 8.2 %collective-permute-start.28 = (f32[13,13,1,128]{3,2,1,0:T(1,128)S(1)}, f32[13,13,1,128]{3,2,1,0:T(1,128)S(1)}, u32[]{:S(2)}, u32[]{:S(2)}) collective-permute-start(f32[13,13,1,128]{3,2,1,0:T(1,128)S(1)} %get-tuple-element.6), channel_id=1, source_target_pairs={{0,1},{1,2},{2,3},{4,5},{5,6},{6,7},{8,9},{9,10},{10,11},{12,13},{... | collective-permute-start | bytes 259592 | tf_op jit(solution)/shard_map/ppermute | solution.py:21
  194.9 7.3 %collective-permute-start.29 = (f32[13,13,1,128]{3,2,1,0:T(1,128)S(1)}, f32[13,13,1,128]{3,2,1,0:T(1,128)S(1)}, u32[]{:S(2)}, u32[]{:S(2)}) collective-permute-start(f32[13,13,1,128]{3,2,1,0:T(1,128)S(1)} %get-tuple-element.7), channel_id=1, source_target_pairs={{1,0},{2,1},{3,2},{5,4},{6,5},{7,6},{9,8},{10,9},{11,10},{13,12},{... | collective-permute-start | bytes 259592 | tf_op jit(solution)/shard_map/ppermute | solution.py:22
  (14 other events, 104.4 us)
where the time goes:
time: 208 us; the launch traced here: 206 us
  starting transfers between devices  87.7 us (42%)
  waiting for transfers between devices  61.9 us (30%)
  local copies, waits for them, and re-layouts  46.3 us (22%)
  other arithmetic  6.82 us (3%)
    ppermute x15, starting transfers between devices, with_halo(): before = lax.ppermute(last, axis, up)  61.6 us
    ppermute x15, waiting for transfers between devices, with_halo(): after = lax.ppermute(leading, axis, down)  60.3 us
    ppermute x15, starting transfers between devices, with_halo(): after = lax.ppermute(leading, axis, down)  26 us
    scatter x5, local copies, waits for them, and re-layouts, assemble(): cube_field = jnp.zeros((NODES ** 3, columns), jnp.float32).at[numbering]....  22.2 us
    gather x5, local copies, waits for them, and re-layouts, assemble(): return joined.reshape(NODES ** 3, columns)[numbering]  8.2 us
    unnamed x28, local copies, waits for them, and re-layouts  5.66 us
  transfers between devices with their start and end apart: 30, of which 19 were waited for; matrix products, arithmetic and copies ran while one was open for 5% of the time, Pallas kernels for 0%

commit v1 on v0

v1 whole, which is shorter than its diff:
```python
import functools
import itertools

import jax
import jax.numpy as jnp
import numpy as np
from jax import lax
from jax.experimental import pallas as pl
from jax.experimental.pallas import tpu as pltpu
from jax.sharding import PartitionSpec as P

NODES = 11
LAST = NODES - 1
AXES = ("gx", "gy", "gz")
MESH = pl.DeviceIdType.MESH

LOW = 0.3
HIGH = 5.0

FACES = [(0, -1, 0), (0, 1, 0), (0, 0, -1), (0, 0, 1), (-1, 0, 0), (1, 0, 0)]
EDGES = [d for d in itertools.product((-1, 0, 1), repeat=3) if sum(map(abs, d)) == 2]
CORNERS = [d for d in itertools.product((-1, 0, 1), repeat=3) if sum(map(abs, d)) == 3]
DIRS = FACES + EDGES + CORNERS
FACE_ROWS, EDGE_ROWS, CORNER_ROWS = 128, 16, 8
EDGE_AT = len(FACES) * FACE_ROWS
CORNER_AT = EDGE_AT + len(EDGES) * EDGE_ROWS
SENT = CORNER_AT + len(CORNERS) * CORNER_ROWS
RIM = 4 * LAST
INNER = FACE_ROWS - RIM
SKEL = 128
PRODUCED = SENT + SKEL
HELD = len(FACES) * INNER + SKEL
SKEL_AT = len(FACES) * INNER
SOURCES = len(FACES) * RIM + SENT - EDGE_AT


def start_of(k):
    if k < 6:
        return k * FACE_ROWS
    if k < 18:
        return EDGE_AT + (k - 6) * EDGE_ROWS
    return CORNER_AT + (k - 18) * CORNER_ROWS


def rows_of(k):
    return FACE_ROWS if k < 6 else EDGE_ROWS if k < 18 else CORNER_ROWS


def nodes_towards(direction):
    spans = [range(NODES) if c == 0 else ((0,) if c < 0 else (LAST,)) for c in direction]
    nodes = list(itertools.product(*spans))
    if sum(map(abs, direction)) == 1:
        free = [i for i in range(3) if direction[i] == 0]
        on_rim = lambda n: any(n[i] in (0, LAST) for i in free)
        nodes = [n for n in nodes if on_rim(n)] + [n for n in nodes if not on_rim(n)]
    return nodes


def tables():
    flat = lambda n: (n[0] * NODES + n[1]) * NODES + n[2]
    outer = lambda n: sum(c in (0, LAST) for c in n)
    skeleton = [n for n in itertools.product(range(NODES), repeat=3) if outer(n) >= 2]
    place = {n: s for s, n in enumerate(skeleton)}
    position = np.full(PRODUCED, -1, np.int32)
    source_of = np.full(SENT, -1, np.int64)
    for k, direction in enumerate(DIRS):
        for j, node in enumerate(nodes_towards(direction)):
            position[start_of(k) + j] = flat(node)
            if node in place:
                source_of[start_of(k) + j] = place[node]
    for s, node in enumerate(skeleton):
        position[SENT + s] = flat(node)
    rows = [start_of(k) + j for k in range(6) for j in range(RIM)] + list(range(EDGE_AT, SENT))
    gather = np.zeros((SKEL, SOURCES), np.float32)
    for column, row in enumerate(rows):
        if source_of[row] >= 0:
            gather[source_of[row], column] = 1.0
    side = np.zeros((3, SKEL), np.int32)
    for s, node in enumerate(skeleton):
        for axis in range(3):
            side[axis, s] = 1 if node[axis] == 0 else 2 if node[axis] == LAST else 0
    position = np.broadcast_to(position[:, None], (PRODUCED, 128))
    side = np.broadcast_to(side[:, :, None], (3, SKEL, 128))
    return position, gather, side


def split(value):
    high = value.astype(jnp.bfloat16)
    low = (value - high.astype(jnp.float32)).astype(jnp.bfloat16)
    return jnp.concatenate([high, low], axis=1)


def dot(a, b, dims=((1,), (0,))):
    return lax.dot_general(a, b, (dims, ((), ())), preferred_element_type=jnp.float32)


def kernel(
    sizes,
    loads_ref,
    schur_hbm,
    dirichlet_hbm,
    order_ref,
    position_ref,
    gather_ref,
    side_ref,
    solution_ref,
    residual_ref,
    schur_raw,
    dirichlet_raw,
    numbers,
    pick,
    half,
    schur,
    dirichlet,
    sent,
    got,
    weight,
    held_residual,
    held_direction,
    send_sem,
    recv_sem,
    load_sem,
):
    count = loads_ref.shape[0]
    get_schur = pltpu.make_async_copy(schur_hbm, schur_raw, load_sem.at[0])
    get_dirichlet = pltpu.make_async_copy(dirichlet_hbm, dirichlet_raw, load_sem.at[1])
    get_dirichlet.start()
    get_schur.start()

    place = [lax.axis_index(axis) for axis in AXES]
    has = {}
    for axis in range(3):
        has[axis, -1] = place[axis] > 0
        has[axis, 1] = place[axis] < sizes[axis] - 1

    def neighbour(direction):
        there, device = None, {}
        for axis in range(3):
            if direction[axis]:
                ok = has[axis, direction[axis]]
                there = ok if there is None else jnp.logical_and(there, ok)
                device[AXES[axis]] = jnp.clip(place[axis] + direction[axis], 0, sizes[axis] - 1)
        return there, device

    neighbours = [neighbour(direction) for direction in DIRS]
    opposite = [DIRS.index(tuple(-c for c in direction)) for direction in DIRS]

    got[...] = jnp.zeros_like(got)
    barrier = pltpu.get_barrier_semaphore()
    for there, device in neighbours:

        @pl.when(there)
        def _():
            pl.semaphore_signal(barrier, inc=1, device_id=device, device_id_type=MESH)

    def copy(k, slot):
        rows = pl.ds(start_of(k), rows_of(k))
        landing = pl.ds(start_of(opposite[k]), rows_of(k))
        return pltpu.make_async_remote_copy(
            src_ref=sent.at[slot, rows],
            dst_ref=got.at[slot, landing],
            send_sem=send_sem.at[slot, k],
            recv_sem=recv_sem.at[slot, opposite[k]],
            device_id=neighbours[k][1],
            device_id_type=MESH,
        )

    def send(slot):
        for k in range(len(DIRS)):

            @pl.when(neighbours[k][0])
            def _():
                copy(k, slot).start()

    def receive(slot):
        for k in range(len(DIRS)):

            @pl.when(neighbours[opposite[k]][0])
            def _():
                copy(k, slot).wait_recv()

    def finish(slot):
        for k in range(len(DIRS)):

            @pl.when(neighbours[k][0])
            def _():
                copy(k, slot).wait_send()

    def assembled(slot):
        parts = []
        for k in range(6):
            rows = pl.ds(start_of(k) + RIM, INNER)
            parts.append(sent[slot, rows, :] + got[slot, rows, :])
        rims = [got[slot, pl.ds(start_of(k), RIM), :] for k in range(6)]
        rims.append(got[slot, pl.ds(EDGE_AT, SENT - EDGE_AT), :])
        both = dot(gather_ref[...], split(jnp.concatenate(rims, axis=0)))
        own = sent[slot, pl.ds(SENT, SKEL), :]
        parts.append(own + (both[:, :128] + both[:, 128:]))
        return jnp.concatenate(parts, axis=0)

    def multiply(matrix, vector, slot):
        for block in range(PRODUCED // 384):
            rows = pl.ds(block * 384, 384)
            sent[slot, rows, :] = dot(matrix[rows, :], vector)

    def renumber(raw, matrix):
        for k in range(6):
            rows = pick[pl.ds(start_of(k) + RIM, INNER), pl.ds(0, count)]
            half[pl.ds(k * INNER, INNER), :] = dot(rows, raw[...]).astype(jnp.bfloat16)
        rows = pick[pl.ds(SENT, SKEL), pl.ds(0, count)]
        half[pl.ds(SKEL_AT, SKEL), :] = dot(rows, raw[...]).astype(jnp.bfloat16)

        def block(i, carry):
            rows = pl.ds(pl.multiple_of(i * 128, 128), 128)
            full = dot(pick[rows, pl.ds(0, count)], half[...], ((1,), (1,)))
            matrix[rows, :] = full.astype(jnp.bfloat16)
            return carry

        lax.fori_loop(0, PRODUCED // 128, block, 0)

    def place_back(value, out_ref):
        both = None
        pair = split(value)
        picks = [(start_of(k) + RIM, INNER, k * INNER) for k in range(6)] + [(SENT, SKEL, SKEL_AT)]
        rows = jnp.concatenate([pick[pl.ds(a, n), pl.ds(0, count)] for a, n, _ in picks], axis=0)
        both = dot(rows, pair, ((0,), (0,)))
        out_ref[...] = both[:, :128] + both[:, 128:]

    numbers[...] = jnp.full_like(numbers, -2)
    numbers[0:1, pl.ds(0, count)] = order_ref[...]
    for lane in range(numbers.shape[1] // 128):
        lanes = pl.ds(lane * 128, 128)
        same = position_ref[...] == numbers[0:1, lanes]
        pick[:, lanes] = same.astype(jnp.float32).astype(jnp.bfloat16)

    pair = split(loads_ref[...])
    for block in range(PRODUCED // 384):
        rows = pl.ds(block * 384, 384)
        both = dot(pick[rows, pl.ds(0, count)], pair)
        sent[0, rows, :] = both[:, :128] + both[:, 128:]

    around = 1
    for axis in range(3):
        around = around * (1 + has[axis, -1].astype(jnp.int32) + has[axis, 1].astype(jnp.int32))
    pl.semaphore_wait(barrier, around - 1)
    send(0)

    share = lambda ok: jnp.where(ok, 2.0, 1.0).astype(jnp.float32)
    for k in range(6):
        axis = [i for i in range(3) if FACES[k][i]][0]
        counted = jnp.full((INNER, 128), share(has[axis, FACES[k][axis]]), jnp.float32)
        weight[pl.ds(k * INNER, INNER), :] = 1.0 / counted
    counted = jnp.ones((SKEL, 128), jnp.float32)
    for axis in range(3):
        side = side_ref[axis]
        low, high = share(has[axis, -1]), share(has[axis, 1])
        counted = counted * jnp.where(side == 1, low, jnp.where(side == 2, high, 1.0))
    weight[pl.ds(SKEL_AT, SKEL), :] = 1.0 / counted

    theta = (HIGH + LOW) / 2.0
    delta = (HIGH - LOW) / 2.0
    sigma = theta / delta
    rho = 1.0 / sigma
    rho_next = 1.0 / (2.0 * sigma - rho)

    get_dirichlet.wait()
    renumber(dirichlet_raw, dirichlet)
    receive(0)
    held_residual[...] = assembled(0)

    multiply(dirichlet, (weight[...] * held_residual[...]).astype(jnp.bfloat16), 1)
    send(1)
    get_schur.wait()
    renumber(schur_raw, schur)
    finish(0)
    receive(1)
    held_direction[...] = weight[...] * assembled(1) / theta

    multiply(schur, held_direction[...].astype(jnp.bfloat16), 0)
    send(0)
    finish(1)
    receive(0)
    held_residual[...] = held_residual[...] - assembled(0)

    multiply(dirichlet, (weight[...] * held_residual[...]).astype(jnp.bfloat16), 1)
    send(1)
    finish(0)
    receive(1)
    former = held_direction[...]
    direction = rho_next * rho * former + (2.0 * rho_next / delta) * (weight[...] * assembled(1))
    held_direction[...] = former + direction

    multiply(schur, direction.astype(jnp.bfloat16), 0)
    send(0)
    place_back(held_direction[...], solution_ref)
    finish(1)
    receive(0)
    place_back(held_residual[...] - assembled(0), residual_ref)
    finish(0)


def on_device(sizes, load_parts, schur_blocks, dirichlet_blocks, node_order):
    count, columns = load_parts.shape[-2:]
    position, gather, side = tables()
    vmem = pl.BlockSpec(memory_space=pltpu.VMEM)
    hbm = pl.BlockSpec(memory_space=pl.ANY)
    padded = -(-count // 128) * 128
    bf16, f32 = jnp.bfloat16, jnp.float32
    out = jax.ShapeDtypeStruct((count, columns), f32)
    solution, residual = pl.pallas_call(
        functools.partial(kernel, sizes),
        out_shape=(out, out),
        in_specs=[vmem, hbm, hbm, vmem, vmem, vmem, vmem],
        out_specs=(vmem, vmem),
        scratch_shapes=[
            pltpu.VMEM((count, count), bf16),
            pltpu.VMEM((count, count), bf16),
            pltpu.VMEM((8, padded), jnp.int32),
            pltpu.VMEM((PRODUCED, padded), bf16),
            pltpu.VMEM((HELD, count), bf16),
            pltpu.VMEM((PRODUCED, HELD), bf16),
            pltpu.VMEM((PRODUCED, HELD), bf16),
            pltpu.VMEM((2, PRODUCED, columns), f32),
            pltpu.VMEM((2, SENT, columns), f32),
            pltpu.VMEM((HELD, columns), f32),
            pltpu.VMEM((HELD, columns), f32),
            pltpu.VMEM((HELD, columns), f32),
            pltpu.SemaphoreType.DMA((2, len(DIRS))),
            pltpu.SemaphoreType.DMA((2, len(DIRS))),
            pltpu.SemaphoreType.DMA((2,)),
        ],
        compiler_params=pltpu.CompilerParams(
            collective_id=0, has_side_effects=True, vmem_limit_bytes=40 << 20
        ),
        name="chebyshev",
    )(
        load_parts.reshape(count, columns),
        schur_blocks.reshape(count, count),
        dirichlet_blocks.reshape(count, count),
        node_order.reshape(1, count),
        jnp.asarray(position),
        jnp.asarray(gather, dtype=bf16),
        jnp.asarray(side),
    )
    return solution.reshape(load_parts.shape), residual.reshape(load_parts.shape)


def solution(mesh):
    sizes = tuple(mesh.shape[axis] for axis in AXES)
    in_specs = (
        P("gx", "gy", "gz", None, None),
        P("gx", "gy", "gz", None, None),
        P("gx", "gy", "gz", None, None),
        P("gx", "gy", "gz", None),
    )
    out_specs = (P("gx", "gy", "gz", None, None), P("gx", "gy", "gz", None, None))
    return jax.shard_map(
        functools.partial(on_device, sizes),
        mesh=mesh,
        in_specs=in_specs,
        out_specs=out_specs,
        check_vma=False,
    )
```

time: 208 us -> 61.3 us (0.29)
  the two profiles are of different devices: /device:TPU:161 before, /device:TPU:41 now
where the time goes in v1:
time: 61.3 us; the launch traced here: 61.1 us
  Pallas kernels  54.5 us (89%)
  local copies, waits for them, and re-layouts  5.84 us (10%)
  between operations  0.7 us (1%)
    pallas_call x1, Pallas kernels, on_device(): pl.pallas_call(functools.partial(kernel, sizes), out_shape=(out, out), in...  54.5 us
    unnamed x15, local copies, waits for them, and re-layouts  5.54 us

profile of v1, /device:TPU:41, one launch (start us, length us, event | category | flops | bytes accessed | tf_op | source)
XLA Modules:
  0.0 61.1 jit_solution(5965423746495115723)
XLA Ops:
  0.6 0.0 copy-start.5
  0.6 0.0 copy-start
  0.7 1.1 %copy.13 = f32[1,1,1,602,128]{4,3,2,1,0:T(8,128)S(1)} copy(f32[1,1,1,602,128]{4,2,3,1,0:T(1,128)} %param.7) | data formatting | bytes 616448
  1.7 0.0 copy-done.5
  1.7 0.0 copy-start.4
  1.7 0.1 jit_solution_.7.side_ref
  1.9 0.6 copy-done.4
  2.4 0.0 copy-start.2
  2.4 0.0 copy-start.3
  2.4 0.2 jit_solution_.6.position_ref
  2.6 0.0 copy-done
  2.7 0.7 %copy-done.2 = bf16[128,496]{1,0:T(8,128)(2,1)S(1)} copy-done((bf16[128,496]{1,0:T(8,128)(2,1)S(1)}, bf16[128,496]{1,0:T(8,128)(2,1)}, u32[]{:S(2)}) %copy-start.2) | copy-done | bytes 127000
  3.3 0.0 copy-done.3
  3.3 0.0 copy-start.1
  3.3 1.1 %copy-done.1 = bf16[1,1,1,602,602]{4,3,2,1,0:T(8,128)(2,1)S(1)} copy-done((bf16[1,1,1,602,602]{4,3,2,1,0:T(8,128)(2,1)S(1)}, bf16[1,1,1,602,602]{4,3,2,1,0:T(8,128)(2,1)}, u32[]{:S(2)}) %copy-start.1) | copy-done | bytes 724832
  4.5 54.5 %chebyshev.1 = (f32[602,128]{1,0:T(8,128)S(1)}, f32[602,128]{1,0:T(8,128)S(1)}) custom-call(f32[602,128]{1,0:T(8,128)S(1)} %bitcast.8, bf16[602,602]{1,0:T(8,128)(2,1)S(1)} %bitcast.9, bf16[602,602]{1,0:T(8,128)(2,1)S(1)} %bitcast.10, s32[1,602]{1,0:T(1,128)S(1)} %bitcast.13, s32[1152,128]{1,0:T(8,128)S(1)} %jit_solution_.6.position_ref, ...), custom_call_target="tpu_custom_call" | custom-call | tf_op jit(solution)/shard_map/chebyshev/pallas_call | solution.py:310
  59.0 1.0 %copy.9 = f32[1,1,1,602,128]{4,2,3,1,0:T(1,128)} copy(f32[1,1,1,602,128]{4,3,2,1,0:T(8,128)S(1)} %bitcast.12) | data formatting | bytes 616448
  60.0 1.0 %copy.10 = f32[1,1,1,602,128]{4,2,3,1,0:T(1,128)} copy(f32[1,1,1,602,128]{4,3,2,1,0:T(8,128)S(1)} %bitcast.11) | data formatting | bytes 616448
Async XLA Ops:
  0.6 1.1 %copy-start.5 = (s32[3,128]{1,0:T(4,128)S(1)}, s32[3,128]{1,0:T(4,128)}, u32[]{:S(2)}) copy-start(s32[3,128]{1,0:T(4,128)} %constant.8.clone) | copy-start | bytes 4612
  0.6 2.0 %copy-start = (bf16[1,1,1,602,602]{4,3,2,1,0:T(8,128)(2,1)S(1)}, bf16[1,1,1,602,602]{4,3,2,1,0:T(8,128)(2,1)}, u32[]{:S(2)}) copy-start(bf16[1,1,1,602,602]{4,3,2,1,0:T(8,128)(2,1)} %param.8) | copy-start | bytes 2174428
  1.7 0.7 %copy-start.4 = (s32[1152]{0:T(1024)S(1)}, s32[1152]{0:T(1024)}, u32[]{:S(2)}) copy-start(s32[1152]{0:T(1024)} %constant.6.clone) | copy-start | bytes 13828
  2.4 0.9 %copy-start.2 = (bf16[128,496]{1,0:T(8,128)(2,1)S(1)}, bf16[128,496]{1,0:T(8,128)(2,1)}, u32[]{:S(2)}) copy-start(bf16[128,496]{1,0:T(8,128)(2,1)} %constant.7.clone.gather_ref) | copy-start | bytes 380932
  2.4 0.9 %copy-start.3 = (s32[1,1,1,602]{3,2,1,0:T(1,128)S(1)}, s32[1,1,1,602]{3,2,1,0:T(1,128)}, u32[]{:S(2)}) copy-start(s32[1,1,1,602]{3,2,1,0:T(1,128)} %param.10) | copy-start | bytes 7228
  3.3 1.1 %copy-start.1 = (bf16[1,1,1,602,602]{4,3,2,1,0:T(8,128)(2,1)S(1)}, bf16[1,1,1,602,602]{4,3,2,1,0:T(8,128)(2,1)}, u32[]{:S(2)}) copy-start(bf16[1,1,1,602,602]{4,3,2,1,0:T(8,128)(2,1)} %param.9) | copy-start | bytes 2174428

commit v2 on v1

--- a/solution.py
+++ b/solution.py
@@ -21,29 +21,33 @@
 EDGES = [d for d in itertools.product((-1, 0, 1), repeat=3) if sum(map(abs, d)) == 2]
 CORNERS = [d for d in itertools.product((-1, 0, 1), repeat=3) if sum(map(abs, d)) == 3]
 DIRS = FACES + EDGES + CORNERS
+EARLY = list(range(18, 26)) + list(range(6, 18)) + [0, 1]
+LATE = [2, 3, 4, 5]
 FACE_ROWS, EDGE_ROWS, CORNER_ROWS = 128, 16, 8
-EDGE_AT = len(FACES) * FACE_ROWS
-CORNER_AT = EDGE_AT + len(EDGES) * EDGE_ROWS
-SENT = CORNER_AT + len(CORNERS) * CORNER_ROWS
+CORNER_AT = 0
+EDGE_AT = CORNER_AT + len(CORNERS) * CORNER_ROWS
+FACE_AT = EDGE_AT + len(EDGES) * EDGE_ROWS
+SENT = FACE_AT + len(FACES) * FACE_ROWS
+EARLY_ROWS = FACE_AT + 2 * FACE_ROWS
 RIM = 4 * LAST
 INNER = FACE_ROWS - RIM
 SKEL = 128
 PRODUCED = SENT + SKEL
 HELD = len(FACES) * INNER + SKEL
 SKEL_AT = len(FACES) * INNER
-SOURCES = len(FACES) * RIM + SENT - EDGE_AT
+SOURCES = len(FACES) * RIM + FACE_AT
 
 
 def start_of(k):
     if k < 6:
-        return k * FACE_ROWS
+        return FACE_AT + k * FACE_ROWS
     if k < 18:
         return EDGE_AT + (k - 6) * EDGE_ROWS
     return CORNER_AT + (k - 18) * CORNER_ROWS
 
 
 def rows_of(k):
-    return FACE_ROWS if k < 6 else EDGE_ROWS if k < 18 else CORNER_ROWS
+    return NODES * NODES if k < 6 else NODES if k < 18 else 1
 
 
 def nodes_towards(direction):
@@ -70,18 +74,19 @@
                 source_of[start_of(k) + j] = place[node]
     for s, node in enumerate(skeleton):
         position[SENT + s] = flat(node)
-    rows = [start_of(k) + j for k in range(6) for j in range(RIM)] + list(range(EDGE_AT, SENT))
+    rows = [start_of(k) + j for k in range(6) for j in range(RIM)] + list(range(FACE_AT))
     gather = np.zeros((SKEL, SOURCES), np.float32)
     for column, row in enumerate(rows):
         if source_of[row] >= 0:
             gather[source_of[row], column] = 1.0
-    side = np.zeros((3, SKEL), np.int32)
+    side = np.zeros((3, SKEL), np.float32)
     for s, node in enumerate(skeleton):
         for axis in range(3):
             side[axis, s] = 1 if node[axis] == 0 else 2 if node[axis] == LAST else 0
-    position = np.broadcast_to(position[:, None], (PRODUCED, 128))
-    side = np.broadcast_to(side[:, :, None], (3, SKEL, 128))
-    return position, gather, side
+    columns = np.zeros((16, 128), np.float32)
+    columns[: PRODUCED // 128] = position.reshape(-1, 128)
+    columns[PRODUCED // 128 : PRODUCED // 128 + 3] = side
+    return columns, gather
 
 
 def split(value):
@@ -96,18 +101,20 @@
 
 def kernel(
     sizes,
-    loads_ref,
+    loads_hbm,
     schur_hbm,
     dirichlet_hbm,
-    order_ref,
-    position_ref,
-    gather_ref,
-    side_ref,
+    order_hbm,
+    columns_hbm,
+    gather_hbm,
     solution_ref,
     residual_ref,
+    loads,
     schur_raw,
     dirichlet_raw,
     numbers,
+    columns,
+    gather,
     pick,
     half,
     schur,
@@ -121,11 +128,22 @@
     recv_sem,
     load_sem,
 ):
-    count = loads_ref.shape[0]
-    get_schur = pltpu.make_async_copy(schur_hbm, schur_raw, load_sem.at[0])
-    get_dirichlet = pltpu.make_async_copy(dirichlet_hbm, dirichlet_raw, load_sem.at[1])
-    get_dirichlet.start()
-    get_schur.start()
+    count = loads.shape[0]
+    fetches = [
+        pltpu.make_async_copy(source, target, load_sem.at[i])
+        for i, (source, target) in enumerate(
+            (
+                (columns_hbm, columns),
+                (order_hbm, numbers),
+                (loads_hbm.at[:, 0, :], loads),
+                (dirichlet_hbm, dirichlet_raw),
+                (gather_hbm, gather),
+                (schur_hbm, schur_raw),
+            )
+        )
+    ]
+    for fetch in fetches:
+        fetch.start()
 
     place = [lax.axis_index(axis) for axis in AXES]
     has = {}
@@ -165,8 +183,8 @@
             device_id_type=MESH,
         )
 
-    def send(slot):
-        for k in range(len(DIRS)):
+    def send(slot, some):
+        for k in some:
 
             @pl.when(neighbours[k][0])
             def _():
@@ -192,16 +210,22 @@
             rows = pl.ds(start_of(k) + RIM, INNER)
             parts.append(sent[slot, rows, :] + got[slot, rows, :])
         rims = [got[slot, pl.ds(start_of(k), RIM), :] for k in range(6)]
-        rims.append(got[slot, pl.ds(EDGE_AT, SENT - EDGE_AT), :])
-        both = dot(gather_ref[...], split(jnp.concatenate(rims, axis=0)))
+        rims.append(got[slot, pl.ds(0, FACE_AT), :])
+        both = dot(gather[...], split(jnp.concatenate(rims, axis=0)))
         own = sent[slot, pl.ds(SENT, SKEL), :]
         parts.append(own + (both[:, :128] + both[:, 128:]))
         return jnp.concatenate(parts, axis=0)
 
+    def produce(rows_of_product, slot):
+        for start, rows, some in ((0, EARLY_ROWS, EARLY), (EARLY_ROWS, SENT - EARLY_ROWS, LATE), (SENT, SKEL, [])):
+            sent[slot, pl.ds(start, rows), :] = rows_of_product(pl.ds(start, rows))
+            if slot == 0 and start == 0 and not started:
+                started.append(True)
+                pl.semaphore_wait(barrier, around - 1)
+            send(slot, some)
+
     def multiply(matrix, vector, slot):
-        for block in range(PRODUCED // 384):
-            rows = pl.ds(block * 384, 384)
-            sent[slot, rows, :] = dot(matrix[rows, :], vector)
+        produce(lambda rows: dot(matrix[rows, :], vector), slot)
 
     def renumber(raw, matrix):
         for k in range(6):
@@ -226,24 +250,30 @@
         both = dot(rows, pair, ((0,), (0,)))
         out_ref[...] = both[:, :128] + both[:, 128:]
 
-    numbers[...] = jnp.full_like(numbers, -2)
-    numbers[0:1, pl.ds(0, count)] = order_ref[...]
-    for lane in range(numbers.shape[1] // 128):
-        lanes = pl.ds(lane * 128, 128)
-        same = position_ref[...] == numbers[0:1, lanes]
-        pick[:, lanes] = same.astype(jnp.float32).astype(jnp.bfloat16)
-
-    pair = split(loads_ref[...])
-    for block in range(PRODUCED // 384):
-        rows = pl.ds(block * 384, 384)
-        both = dot(pick[rows, pl.ds(0, count)], pair)
-        sent[0, rows, :] = both[:, :128] + both[:, 128:]
-
     around = 1
     for axis in range(3):
         around = around * (1 + has[axis, -1].astype(jnp.int32) + has[axis, 1].astype(jnp.int32))
-    pl.semaphore_wait(barrier, around - 1)
-    send(0)
+    started = []
+
+    fetches[0].wait()
+    fetches[1].wait()
+    upright = lambda row: jnp.broadcast_to(columns[pl.ds(row, 1), :], (128, 128)).T
+    own = numbers[...].astype(jnp.float32)
+    for block in range(PRODUCED // 128):
+        position = upright(block)
+        for at in range(0, count, 128):
+            width = min(128, count - at)
+            same = position[:, :width] == own[:, at : at + width]
+            pick[pl.ds(block * 128, 128), pl.ds(at, width)] = same.astype(jnp.float32).astype(jnp.bfloat16)
+
+    fetches[2].wait()
+    pair = split(loads[...])
+
+    def first_rows(rows):
+        both = dot(pick[rows, pl.ds(0, count)], pair)
+        return both[:, :128] + both[:, 128:]
+
+    produce(first_rows, 0)
 
     share = lambda ok: jnp.where(ok, 2.0, 1.0).astype(jnp.float32)
     for k in range(6):
@@ -252,7 +282,7 @@
         weight[pl.ds(k * INNER, INNER), :] = 1.0 / counted
     counted = jnp.ones((SKEL, 128), jnp.float32)
     for axis in range(3):
-        side = side_ref[axis]
+        side = upright(PRODUCED // 128 + axis)
         low, high = share(has[axis, -1]), share(has[axis, 1])
         counted = counted * jnp.where(side == 1, low, jnp.where(side == 2, high, 1.0))
     weight[pl.ds(SKEL_AT, SKEL), :] = 1.0 / counted
@@ -263,27 +293,25 @@
     rho = 1.0 / sigma
     rho_next = 1.0 / (2.0 * sigma - rho)
 
-    get_dirichlet.wait()
+    fetches[3].wait()
+    fetches[4].wait()
     renumber(dirichlet_raw, dirichlet)
     receive(0)
     held_residual[...] = assembled(0)
 
     multiply(dirichlet, (weight[...] * held_residual[...]).astype(jnp.bfloat16), 1)
-    send(1)
-    get_schur.wait()
+    fetches[5].wait()
     renumber(schur_raw, schur)
     finish(0)
     receive(1)
     held_direction[...] = weight[...] * assembled(1) / theta
 
     multiply(schur, held_direction[...].astype(jnp.bfloat16), 0)
-    send(0)
     finish(1)
     receive(0)
     held_residual[...] = held_residual[...] - assembled(0)
 
     multiply(dirichlet, (weight[...] * held_residual[...]).astype(jnp.bfloat16), 1)
-    send(1)
     finish(0)
     receive(1)
     former = held_direction[...]
@@ -291,7 +319,6 @@
     held_direction[...] = former + direction
 
     multiply(schur, direction.astype(jnp.bfloat16), 0)
-    send(0)
     place_back(held_direction[...], solution_ref)
     finish(1)
     receive(0)
@@ -299,24 +326,37 @@
     finish(0)
 
 
+def hand_out(solution_in, residual_in, solution_out, residual_out, sem):
+    copies = [
+        pltpu.make_async_copy(solution_in, solution_out.at[:, 0, :], sem.at[0]),
+        pltpu.make_async_copy(residual_in, residual_out.at[:, 0, :], sem.at[1]),
+    ]
+    for copy in copies:
+        copy.start()
+    for copy in copies:
+        copy.wait()
+
+
 def on_device(sizes, load_parts, schur_blocks, dirichlet_blocks, node_order):
     count, columns = load_parts.shape[-2:]
-    position, gather, side = tables()
+    table, gather = tables()
     vmem = pl.BlockSpec(memory_space=pltpu.VMEM)
     hbm = pl.BlockSpec(memory_space=pl.ANY)
-    padded = -(-count // 128) * 128
     bf16, f32 = jnp.bfloat16, jnp.float32
     out = jax.ShapeDtypeStruct((count, columns), f32)
     solution, residual = pl.pallas_call(
         functools.partial(kernel, sizes),
         out_shape=(out, out),
-        in_specs=[vmem, hbm, hbm, vmem, vmem, vmem, vmem],
+        in_specs=[hbm] * 6,
         out_specs=(vmem, vmem),
         scratch_shapes=[
+            pltpu.VMEM((count, columns), f32),
             pltpu.VMEM((count, count), bf16),
             pltpu.VMEM((count, count), bf16),
-            pltpu.VMEM((8, padded), jnp.int32),
-            pltpu.VMEM((PRODUCED, padded), bf16),
+            pltpu.VMEM((1, count), jnp.int32),
+            pltpu.VMEM((16, 128), f32),
+            pltpu.VMEM((SKEL, SOURCES), bf16),
+            pltpu.VMEM((PRODUCED, count), bf16),
             pltpu.VMEM((HELD, count), bf16),
             pltpu.VMEM((PRODUCED, HELD), bf16),
             pltpu.VMEM((PRODUCED, HELD), bf16),
@@ -327,21 +367,29 @@
             pltpu.VMEM((HELD, columns), f32),
             pltpu.SemaphoreType.DMA((2, len(DIRS))),
             pltpu.SemaphoreType.DMA((2, len(DIRS))),
-            pltpu.SemaphoreType.DMA((2,)),
+            pltpu.SemaphoreType.DMA((6,)),
         ],
         compiler_params=pltpu.CompilerParams(
-            collective_id=0, has_side_effects=True, vmem_limit_bytes=40 << 20
+            collective_id=0, has_side_effects=True, vmem_limit_bytes=60 << 20
         ),
         name="chebyshev",
     )(
-        load_parts.reshape(count, columns),
+        load_parts.reshape(count, 1, columns),
         schur_blocks.reshape(count, count),
         dirichlet_blocks.reshape(count, count),
         node_order.reshape(1, count),
-        jnp.asarray(position),
+        jnp.asarray(table),
         jnp.asarray(gather, dtype=bf16),
-        jnp.asarray(side),
     )
+    out = jax.ShapeDtypeStruct((count, 1, columns), f32)
+    solution, residual = pl.pallas_call(
+        hand_out,
+        out_shape=(out, out),
+        in_specs=[vmem, vmem],
+        out_specs=(hbm, hbm),
+        scratch_shapes=[pltpu.SemaphoreType.DMA((2,))],
+        name="hand_out",
+    )(solution, residual)
     return solution.reshape(load_parts.shape), residual.reshape(load_parts.shape)
 
 

time: 61.3 us -> 51.7 us (0.84)
  the two profiles are of different devices: /device:TPU:41 before, /device:TPU:9 now
where the time goes in v2:
time: 51.7 us; the launch traced here: 51.5 us
  Pallas kernels  50.9 us (98%)
  between operations  0.64 us (1%)
    pallas_call x1, Pallas kernels, on_device(): pl.pallas_call(functools.partial(kernel, sizes), out_shape=(out, out), in...  49 us
    pallas_call x1, Pallas kernels, on_device(): pl.pallas_call(hand_out, out_shape=(out, out), in_specs=[vmem, vmem], out...  1.9 us

profile of v2, /device:TPU:9, one launch (start us, length us, event | category | flops | bytes accessed | tf_op | source)
XLA Modules:
  0.0 51.5 jit_solution(17843461279361541667)
XLA Ops:
  0.6 49.0 %chebyshev.1 = (f32[602,128]{1,0:T(8,128)}, f32[602,128]{1,0:T(8,128)}) custom-call(f32[602,1,128]{2,1,0:T(1,128)} %bitcast.12, bf16[602,602]{1,0:T(8,128)(2,1)} %bitcast.10, bf16[602,602]{1,0:T(8,128)(2,1)} %bitcast.11, s32[1,602]{1,0:T(1,128)} %bitcast.13, f32[16,128]{1,0:T(8,128)} %constant.4.clone.columns_hbm, bf16[128,496]{1,0:T(8,128)(2,1)} %constant.5.clone.gather_hbm), custom_call_target="tpu_custom_call" | custom-call | tf_op jit(solution)/shard_map/chebyshev/pallas_call | solution.py:347
  49.6 1.9 %hand_out.1 = (f32[602,1,128]{2,1,0:T(1,128)}, f32[602,1,128]{2,1,0:T(1,128)}) custom-call(f32[602,128]{1,0:T(8,128)} %get-tuple-element.6.solution_in, f32[602,128]{1,0:T(8,128)} %get-tuple-element.7.residual_in), custom_call_target="tpu_custom_call" | custom-call | tf_op jit(solution)/shard_map/hand_out/pallas_call | solution.py:385

commit v3 on v2

--- a/solution.py
+++ b/solution.py
@@ -21,8 +21,10 @@
 EDGES = [d for d in itertools.product((-1, 0, 1), repeat=3) if sum(map(abs, d)) == 2]
 CORNERS = [d for d in itertools.product((-1, 0, 1), repeat=3) if sum(map(abs, d)) == 3]
 DIRS = FACES + EDGES + CORNERS
-EARLY = list(range(18, 26)) + list(range(6, 18)) + [0, 1]
+SMALL = sorted(range(6, 26), key=lambda k: ((0, 1, -1).index(DIRS[k][2]) == 0, DIRS[k][2], -k))
+EARLY = SMALL + [0, 1]
 LATE = [2, 3, 4, 5]
+ARRIVING = SMALL + [4, 5, 2, 3, 0, 1]
 FACE_ROWS, EDGE_ROWS, CORNER_ROWS = 128, 16, 8
 CORNER_AT = 0
 EDGE_AT = CORNER_AT + len(CORNERS) * CORNER_ROWS
@@ -116,6 +118,7 @@
     columns,
     gather,
     pick,
+    held_pick,
     half,
     schur,
     dirichlet,
@@ -183,26 +186,37 @@
             device_id_type=MESH,
         )
 
+    inner = functools.reduce(jnp.logical_and, [has[axis, way] for axis in (0, 1) for way in (-1, 1)])
+
+    def each(some, act):
+        @pl.when(inner)
+        def _():
+            for way, run in itertools.groupby(some, lambda k: DIRS[k][2]):
+                run = list(run)
+                if way == 0:
+                    for k in run:
+                        act(k)
+                else:
+
+                    @pl.when(has[2, way])
+                    def _():
+                        for k in run:
+                            act(k)
+
+        @pl.when(jnp.logical_not(inner))
+        def _():
+            for k in some:
+                pl.when(neighbours[k][0])(functools.partial(act, k))
+
     def send(slot, some):
-        for k in some:
-
-            @pl.when(neighbours[k][0])
-            def _():
-                copy(k, slot).start()
+        if some:
+            each(some, lambda k: copy(k, slot).start())
 
     def receive(slot):
-        for k in range(len(DIRS)):
-
-            @pl.when(neighbours[opposite[k]][0])
-            def _():
-                copy(k, slot).wait_recv()
+        each(ARRIVING, lambda k: copy(opposite[k], slot).wait_recv())
 
     def finish(slot):
-        for k in range(len(DIRS)):
-
-            @pl.when(neighbours[k][0])
-            def _():
-                copy(k, slot).wait_send()
+        each(ARRIVING, lambda k: copy(k, slot).wait_send())
 
     def assembled(slot):
         parts = []
@@ -228,26 +242,15 @@
         produce(lambda rows: dot(matrix[rows, :], vector), slot)
 
     def renumber(raw, matrix):
-        for k in range(6):
-            rows = pick[pl.ds(start_of(k) + RIM, INNER), pl.ds(0, count)]
-            half[pl.ds(k * INNER, INNER), :] = dot(rows, raw[...]).astype(jnp.bfloat16)
-        rows = pick[pl.ds(SENT, SKEL), pl.ds(0, count)]
-        half[pl.ds(SKEL_AT, SKEL), :] = dot(rows, raw[...]).astype(jnp.bfloat16)
-
-        def block(i, carry):
-            rows = pl.ds(pl.multiple_of(i * 128, 128), 128)
-            full = dot(pick[rows, pl.ds(0, count)], half[...], ((1,), (1,)))
-            matrix[rows, :] = full.astype(jnp.bfloat16)
-            return carry
-
-        lax.fori_loop(0, PRODUCED // 128, block, 0)
+        for at in range(0, count, 256):
+            lanes = pl.ds(at, min(256, count - at))
+            half[:, lanes] = dot(held_pick[...], raw[:, lanes]).astype(jnp.bfloat16)
+        for at in range(0, HELD, 256):
+            lanes = pl.ds(at, min(256, HELD - at))
+            matrix[:, lanes] = dot(pick[...], half[lanes, :], ((1,), (1,))).astype(jnp.bfloat16)
 
     def place_back(value, out_ref):
-        both = None
-        pair = split(value)
-        picks = [(start_of(k) + RIM, INNER, k * INNER) for k in range(6)] + [(SENT, SKEL, SKEL_AT)]
-        rows = jnp.concatenate([pick[pl.ds(a, n), pl.ds(0, count)] for a, n, _ in picks], axis=0)
-        both = dot(rows, pair, ((0,), (0,)))
+        both = dot(held_pick[...], split(value), ((0,), (0,)))
         out_ref[...] = both[:, :128] + both[:, 128:]
 
     around = 1
@@ -259,21 +262,25 @@
     fetches[1].wait()
     upright = lambda row: jnp.broadcast_to(columns[pl.ds(row, 1), :], (128, 128)).T
     own = numbers[...].astype(jnp.float32)
-    for block in range(PRODUCED // 128):
-        position = upright(block)
-        for at in range(0, count, 128):
-            width = min(128, count - at)
-            same = position[:, :width] == own[:, at : at + width]
-            pick[pl.ds(block * 128, 128), pl.ds(at, width)] = same.astype(jnp.float32).astype(jnp.bfloat16)
-
-    fetches[2].wait()
-    pair = split(loads[...])
+    pair = []
 
     def first_rows(rows):
-        both = dot(pick[rows, pl.ds(0, count)], pair)
+        for block in range(rows.start // 128, (rows.start + rows.size) // 128):
+            position = upright(block)
+            for at in range(0, count, 128):
+                width = min(128, count - at)
+                same = position[:, :width] == own[:, at : at + width]
+                pick[pl.ds(block * 128, 128), pl.ds(at, width)] = same.astype(jnp.float32).astype(jnp.bfloat16)
+        if not pair:
+            fetches[2].wait()
+            pair.append(split(loads[...]))
+        both = dot(pick[rows, pl.ds(0, count)], pair[0])
         return both[:, :128] + both[:, 128:]
 
     produce(first_rows, 0)
+    for k in range(6):
+        held_pick[pl.ds(k * INNER, INNER), :] = pick[pl.ds(start_of(k) + RIM, INNER), :]
+    held_pick[pl.ds(SKEL_AT, SKEL), :] = pick[pl.ds(SENT, SKEL), :]
 
     share = lambda ok: jnp.where(ok, 2.0, 1.0).astype(jnp.float32)
     for k in range(6):
@@ -357,6 +364,7 @@
             pltpu.VMEM((16, 128), f32),
             pltpu.VMEM((SKEL, SOURCES), bf16),
             pltpu.VMEM((PRODUCED, count), bf16),
+            pltpu.VMEM((HELD, count), bf16),
             pltpu.VMEM((HELD, count), bf16),
             pltpu.VMEM((PRODUCED, HELD), bf16),
             pltpu.VMEM((PRODUCED, HELD), bf16),

time: 51.7 us -> 51.5 us (level)
  no operation moved by 1% of the time
where the time goes in v3:
time: 51.5 us; the launch traced here: 51.3 us
  Pallas kernels  50.7 us (98%)
  between operations  0.64 us (1%)
    pallas_call x1, Pallas kernels, on_device(): pl.pallas_call(functools.partial(kernel, sizes), out_shape=(out, out), in...  48.8 us
    pallas_call x1, Pallas kernels, on_device(): pl.pallas_call(hand_out, out_shape=(out, out), in_specs=[vmem, vmem], out...  1.9 us

profile of v3, /device:TPU:9, one launch (start us, length us, event | category | flops | bytes accessed | tf_op | source)
XLA Modules:
  0.0 51.3 jit_solution(15674088322730045298)
XLA Ops:
  0.6 48.8 %chebyshev.1 = (f32[602,128]{1,0:T(8,128)}, f32[602,128]{1,0:T(8,128)}) custom-call(f32[602,1,128]{2,1,0:T(1,128)} %bitcast.12, bf16[602,602]{1,0:T(8,128)(2,1)} %bitcast.10, bf16[602,602]{1,0:T(8,128)(2,1)} %bitcast.11, s32[1,602]{1,0:T(1,128)} %bitcast.13, f32[16,128]{1,0:T(8,128)} %constant.4.clone.columns_hbm, bf16[128,496]{1,0:T(8,128)(2,1)} %constant.5.clone.gather_hbm), custom_call_target="tpu_custom_call" | custom-call | tf_op jit(solution)/shard_map/chebyshev/pallas_call | solution.py:354
  49.4 1.9 %hand_out.1 = (f32[602,1,128]{2,1,0:T(1,128)}, f32[602,1,128]{2,1,0:T(1,128)}) custom-call(f32[602,128]{1,0:T(8,128)} %get-tuple-element.6.solution_in, f32[602,128]{1,0:T(8,128)} %get-tuple-element.7.residual_in), custom_call_target="tpu_custom_call" | custom-call | tf_op jit(solution)/shard_map/hand_out/pallas_call | solution.py:393
